TPU v7x, 128 devices: a whole 4x4x4 slice. The times are simulated.
128 devices in a mesh: rows: 32 (over z, x, core), cols: 4 (over y).
Axes of the slice: x: 4, y: 4, z: 4, core: 2. Of those that a mesh axis runs over, the one named last changes fastest.
Arguments:
- panel_cols: float32 [262144, 256], P(('rows', 'cols')), may hold values from -10000 to 10000, as said below
- trailing: float32 [262144, 1024], P('rows', 'cols'), may hold values from -200000 to 200000
Outputs:
- r_factor: float32 [256, 256], replicated
- r_cross: float32 [256, 1024], P(None, 'cols')
- updated: float32 [262144, 1024], P('rows', 'cols')
Inputs may be any that keep to these rules, and one draw needn't show every extreme that they name: panel_cols has full column rank.
All inputs are finite; a program needn't handle non-finite values.
Results may differ from a plain program's by a relative error of at most 0.0003.
Values sent between devices are 32-bit elements; how exact they have to be, the bound alone decides.
No kernel may reach another device: no remote copies, remote signals or barrier semaphores. Data moves between devices by JAX's collectives and lax.ppermute only.
A program may use at most 128 MiB of HBM per device.

v0:
```python
import math
import jax
import jax.numpy as jnp
from jax import lax
from jax.sharding import PartitionSpec as P


def matmul(left, right):
    return jnp.dot(left, right, precision=lax.Precision.HIGHEST)


def lower_factor(gram_sum):
    return jnp.linalg.cholesky(gram_sum)


def lower_inverse(lower):
    identity = jnp.eye(lower.shape[0], dtype=jnp.float32)
    return jax.scipy.linalg.solve_triangular(lower, identity, lower=True)


def local(panel_cols, trailing):
    rows_total = trailing.shape[0] * lax.axis_size("rows")
    shrink = 1.0 / math.sqrt(rows_total)
    gram_sum = lax.psum(matmul(panel_cols.T, panel_cols), ("rows", "cols"))
    lower = lower_factor(gram_sum)
    inverse = lower_inverse(lower)
    basis_part = matmul(panel_cols, inverse.T)
    orthonormal = lax.all_gather(basis_part, "cols", axis=0, tiled=True)
    coupling = lax.psum(matmul(orthonormal.T, trailing), "rows")
    updated = trailing - matmul(orthonormal, coupling)
    return (lower.T * shrink, coupling * shrink, updated)


def solution(mesh):
    in_specs = (P(("rows", "cols"), None), P("rows", "cols"))
    out_specs = (P(), P(None, "cols"), P("rows", "cols"))
    return jax.shard_map(local, mesh=mesh, in_specs=in_specs, out_specs=out_specs, check_vma=False)
```

profile of v0, /device:TPU:1, one launch (start us, length us, event | category | flops | bytes accessed | tf_op | source)
XLA Modules:
  0.0 447.2 jit_solution(1440533770498955808)
XLA Ops:
  7.2 1.5 copy-done
  8.8 4.2 fusion.14
  13.2 145.0 %all-reduce.4.cloned.1.call-done = f32[256,256]{0,1:T(8,128)} async-done(((f32[256,256]{0,1:T(8,128)}), f32[256,256]{0,1:T(8,128)}) %all-reduce.4.cloned.1.call-update) | async-done | bytes 262160 | tf_op jit(solution)/shard_map/psum | solution.py:24
  158.2 1.1 copy.6
  159.3 1.0 fusion.3
  160.3 11.7 %cholesky.50 = f32[128,128]{1,0:T(8,128)S(1)} custom-call(f32[128,128]{1,0:T(8,128)S(1)} %cholesky.118), custom_call_target="Cholesky" | custom-call | tf_op jit(solution)/shard_map/jit(cholesky)/cholesky | solution.py:13
  172.0 9.8 %custom-call.15 = f32[1,128,128]{1,2,0:T(8,128)S(1)} custom-call(f32[1,128,128]{2,1,0:T(8,128)S(1)} %get-tuple-element.29), custom_call_target="InvertDiagBlocksLowerTriangular" | custom-call | tf_op jit(solution)/shard_map/jit(cholesky)/cholesky | solution.py:13
  182.1 0.3 convolution_subtract_fusion.2
  182.3 11.7 %cholesky.105 = f32[128,128]{1,0:T(8,128)S(1)} custom-call(f32[128,128]{1,0:T(8,128)S(1)} %convolution_subtract_fusion.2), custom_call_target="Cholesky" | custom-call | tf_op jit(solution)/shard_map/jit(cholesky)/cholesky | solution.py:13
  194.1 0.6 compare_reduce_fusion
  196.2 4.2 while.1
  196.3 0.6 fusion.28
  196.9 1.4 bitcast_dynamic-update-slice_fusion.2
  198.3 0.6 fusion.28
  198.9 1.4 bitcast_dynamic-update-slice_fusion.2
  200.3 19.7 %custom-call.16 = f32[2,128,128]{1,2,0:T(8,128)S(1)} custom-call(f32[2,128,128]{2,1,0:T(8,128)S(1)} %get-tuple-element.10), custom_call_target="InvertDiagBlocksLowerTriangular" | custom-call | tf_op jit(solution)/shard_map/jit(_solve_triangular)/triangular_solve | solution.py:18
  220.6 0.3 fusion.8
  220.9 3.3 convolution_bitcast_fusion
  224.2 80.6 %all-gather.2.cloned.1.call-done = f32[8192,256]{0,1:T(8,128)} async-done(((f32[2048,256]{0,1:T(8,128)}), f32[8192,256]{0,1:T(8,128)}) %all-gather.2.cloned.1.call-update) | async-done | bytes 8388624 | tf_op jit(solution)/shard_map/all_gather | solution.py:28
  304.8 11.4 %fusion.15 = f32[256,256]{1,0:T(8,128)} fusion(f32[8192,256]{0,1:T(8,128)} %all-gather.2.cloned.1.call-done, f32[8192,256]{1,0:T(8,128)} %param.3), kind=kOutput, calls=%fused_computation.39 | convolution fusion | flops 6442450944 | bytes 17039360 | tf_op jit(solution)/shard_map/dot_general | solution.py:9
  316.2 0.8 copy.7
  317.1 101.8 %all-reduce.6.cloned.1.call-done = f32[256,256]{1,0:T(8,128)} async-done(((f32[256,256]{1,0:T(8,128)}), f32[256,256]{1,0:T(8,128)}) %all-reduce.6.cloned.1.call-update) | async-done | bytes 262160 | tf_op jit(solution)/shard_map/psum | solution.py:29
  418.9 21.1 %convolution_subtract_fusion = f32[8192,256]{1,0:T(8,128)} fusion(f32[8192,256]{1,0:T(8,128)} %param.3, f32[8192,256]{0,1:T(8,128)} %all-gather.2.cloned.1.call-done, f32[256,256]{1,0:T(8,128)} %all-reduce.6.cloned.1.call-done), kind=kOutput, calls=%fused_computation.2 | convolution fusion | flops 6444548096 | bytes 25427968 | tf_op jit(solution)/shard_map/dot_general | solution.py:9
  440.0 0.7 broadcast_multiply_fusion
  (23 shorter events, 1.3 us)
Async XLA Ops:
  7.2 1.6 copy-start
  7.2 151.0 %all-reduce.4.cloned.1.call-start = ((), (), s32[]{:S(2)}) async-start(), calls=%async_computation | async-start | bytes 524288 | tf_op jit(solution)/shard_map/psum | solution.py:24
  12.9 291.9 %all-gather.2.cloned.1.call-start = ((), (), s32[]{:S(2)}) async-start(), calls=%async_computation.1 | async-start | bytes 10485760 | tf_op jit(solution)/shard_map/all_gather | solution.py:28
  224.2 194.7 %all-reduce.6.cloned.1.call-start = ((), (), s32[]{:S(2)}) async-start(), calls=%async_computation.2 | async-start | bytes 524288 | tf_op jit(solution)/shard_map/psum | solution.py:29
  418.9 21.1 %copy-start.1 = (f32[256,256]{1,0:T(8,128)S(1)}, f32[256,256]{1,0:T(8,128)}, u32[]{:S(2)}) copy-start(f32[256,256]{1,0:T(8,128)} %all-reduce.6.cloned.1.call-done) | copy-start | bytes 786436
Sparse Core Ops, SparseCore 0:
  13.3 144.8 all-reduce.3
  224.3 80.4 all-gather.1
  316.4 102.4 all-reduce.5
where the time goes:
time: 447 us
  waiting for transfers between devices  327 us (73%)
  other arithmetic  55.4 us (12%)
  matrix products  41.2 us (9%)
  between operations  15.2 us (3%)
  local copies, waits for them, and re-layouts  7.51 us (2%)
    psum x1, waiting for transfers between devices, local(): gram_sum = lax.psum(matmul(panel_cols.T, panel_cols), ('rows', 'cols'))  145 us
    psum x1, waiting for transfers between devices, local(): coupling = lax.psum(matmul(orthonormal.T, trailing), 'rows')  102 us
    all_gather x1, waiting for transfers between devices, local(): orthonormal = lax.all_gather(basis_part, 'cols', axis=0, tiled=True)  80.6 us
    dot_general x4, matrix products, matmul(): return jnp.dot(left, right, precision=lax.Precision.HIGHEST)  39.9 us
    another operation x6, other arithmetic, lower_factor(): return jnp.linalg.cholesky(gram_sum)  34 us
    another operation x3, other arithmetic, lower_inverse(): return jax.scipy.linalg.solve_triangular(lower, identity, lower=True)  19.7 us
  transfers between devices with their start and end apart: 3, of which 3 were waited for; matrix products, arithmetic and copies ran while one was open for 0% of the time, Pallas kernels for 0%

commit v1 on v0

--- a/solution.py
+++ b/solution.py
@@ -25,7 +25,9 @@
     lower = lower_factor(gram_sum)
     inverse = lower_inverse(lower)
     basis_part = matmul(panel_cols, inverse.T)
-    orthonormal = lax.all_gather(basis_part, "cols", axis=0, tiled=True)
+    orthonormal = jnp.concatenate(
+        lax.all_to_all(jnp.stack(lax.axis_size("cols") * [basis_part]), "cols", 0, 0), axis=0
+    )
     coupling = lax.psum(matmul(orthonormal.T, trailing), "rows")
     updated = trailing - matmul(orthonormal, coupling)
     return (lower.T * shrink, coupling * shrink, updated)

time: 447 us -> 482 us (1.078)
  blocking collectives: 0 us -> 96.6 us
  waiting for transfers between devices: 327 us -> 244 us
  loops' own time: 0.21 us -> 12.4 us
  local copies, waits for them, and re-layouts: 7.51 us -> 16.1 us
    all_to_all x0 -> x1, blocking collectives: none -> 96.6 us  [local(): lax.all_to_all(jnp.stack(lax.axis_size('cols') * [basis_part]), 'cols', 0...]
    all_gather x1 -> x0, waiting for transfers between devices: 80.6 us -> none  [local(): orthonormal = lax.all_gather(basis_part, 'cols', axis=0, tiled=True)]
    another operation x1, loops' own time: 0.21 us -> 12.4 us  [lower_inverse(): return jax.scipy.linalg.solve_triangular(lower, identity, lower=True)]
  transfers between devices with their start and end apart: 3 -> 2, of which waited for: 3 -> 2; matrix products, arithmetic and copies ran while one was open for 0% -> 0% of each run, Pallas kernels for 0% -> 0%
where the time goes in v1:
time: 482 us; the launch traced here: 478 us
  waiting for transfers between devices  244 us (51%)
  blocking collectives  96.6 us (20%)
  other arithmetic  55.4 us (11%)
  matrix products  37.9 us (8%)
  local copies, waits for them, and re-layouts  16.1 us (3%)
  between operations  15.7 us (3%)
  loops' own time  12.4 us (3%)
    psum x1, waiting for transfers between devices, local(): gram_sum = lax.psum(matmul(panel_cols.T, panel_cols), ('rows', 'cols'))  145 us
    psum x1, waiting for transfers between devices, local(): coupling = lax.psum(matmul(orthonormal.T, trailing), 'rows')  98.9 us
    all_to_all x1, blocking collectives, local(): lax.all_to_all(jnp.stack(lax.axis_size('cols') * [basis_part]), 'cols', 0...  96.6 us
    dot_general x4, matrix products, matmul(): return jnp.dot(left, right, precision=lax.Precision.HIGHEST)  36.6 us
    another operation x6, other arithmetic, lower_factor(): return jnp.linalg.cholesky(gram_sum)  34 us
    another operation x3, other arithmetic, lower_inverse(): return jax.scipy.linalg.solve_triangular(lower, identity, lower=True)  19.7 us
    another operation x1, loops' own time, lower_inverse(): return jax.scipy.linalg.solve_triangular(lower, identity, lower=True)  12.4 us
  transfers between devices with their start and end apart: 2, of which 2 were waited for; matrix products, arithmetic and copies ran while one was open for 0% of the time, Pallas kernels for 0%

profile of v1, /device:TPU:1, one launch (start us, length us, event | category | flops | bytes accessed | tf_op | source)
XLA Modules:
  0.0 478.2 jit_solution(4305613524410411497)
XLA Ops:
  7.2 1.5 copy-done
  8.8 4.2 fusion.14
  13.4 144.8 %all-reduce.4.cloned.1.call-done = f32[256,256]{0,1:T(8,128)} async-done(((f32[256,256]{0,1:T(8,128)}), f32[256,256]{0,1:T(8,128)}) %all-reduce.4.cloned.1.call-update) | async-done | bytes 262160 | tf_op jit(solution)/shard_map/psum | solution.py:24
  158.2 1.1 copy.6
  159.3 1.0 fusion.3
  160.3 11.7 %cholesky.50 = f32[128,128]{1,0:T(8,128)S(1)} custom-call(f32[128,128]{1,0:T(8,128)S(1)} %cholesky.118), custom_call_target="Cholesky" | custom-call | tf_op jit(solution)/shard_map/jit(cholesky)/cholesky | solution.py:13
  172.0 9.8 %custom-call.15 = f32[1,128,128]{1,2,0:T(8,128)S(1)} custom-call(f32[1,128,128]{2,1,0:T(8,128)S(1)} %get-tuple-element.29), custom_call_target="InvertDiagBlocksLowerTriangular" | custom-call | tf_op jit(solution)/shard_map/jit(cholesky)/cholesky | solution.py:13
  182.3 11.7 %cholesky.105 = f32[128,128]{1,0:T(8,128)S(1)} custom-call(f32[128,128]{1,0:T(8,128)S(1)} %convolution_subtract_fusion.2), custom_call_target="Cholesky" | custom-call | tf_op jit(solution)/shard_map/jit(cholesky)/cholesky | solution.py:13
  194.1 0.6 compare_reduce_fusion
  196.2 16.3 %while.1 = (s32[]{:T(128)}, f32[256,256]{1,0:T(8,128)S(1)}, s32[2,2]{1,0:T(2,128)S(1)}, f32[2,128,128]{2,1,0:T(8,128)S(1)}, s32[]{:T(128)}) while((s32[]{:T(128)}, f32[256,256]{1,0:T(8,128)S(1)}, s32[2,2]{1,0:T(2,128)S(1)}, f32[2,128,128]{2,1,0:T(8,128)S(1)}, s32[]{:T(128)}) %tuple.29), condition=%wide.while_cond, body=%wide.while_body.sunk | while | flops 2 | bytes 131189 | solution.py:18
  208.5 0.6 fusion.28
  209.1 1.4 bitcast_dynamic-update-slice_fusion.2
  211.1 1.4 bitcast_dynamic-update-slice_fusion.2
  212.5 19.7 %custom-call.16 = f32[2,128,128]{1,2,0:T(8,128)S(1)} custom-call(f32[2,128,128]{2,1,0:T(8,128)S(1)} %get-tuple-element.10), custom_call_target="InvertDiagBlocksLowerTriangular" | custom-call | tf_op jit(solution)/shard_map/jit(_solve_triangular)/triangular_solve | solution.py:18
  233.0 3.3 convolution_bitcast_fusion
  236.3 2.9 copy.7
  239.2 2.4 stack.2
  241.6 96.6 %all_to_all.5 = f32[4,2048,256]{2,1,0:T(8,128)S(1)} all-to-all(f32[4,2048,256]{2,1,0:T(8,128)S(1)} %stack.2), channel_id=1, replica_groups=mesh['rows'=32,'cols'=4] {'cols'}, dimensions={0} | all-to-all | bytes 16777216 | tf_op jit(solution)/shard_map/all_to_all | solution.py:29
  338.2 3.2 copy-done.1
  341.4 14.7 %fusion.15 = f32[256,256]{1,0:T(8,128)} fusion(f32[8192,256]{1,0:T(8,128)S(1)} %bitcast.43, f32[8192,256]{1,0:T(8,128)S(1)} %bitcast.46), kind=kOutput, calls=%fused_computation.39 | convolution fusion | flops 6442450944 | bytes 17039360 | tf_op jit(solution)/shard_map/dot_general | solution.py:9
  356.2 0.8 copy.8
  357.0 98.9 %all-reduce.6.cloned.1.call-done = f32[256,256]{1,0:T(8,128)} async-done(((f32[256,256]{1,0:T(8,128)}), f32[256,256]{1,0:T(8,128)}) %all-reduce.6.cloned.1.call-update) | async-done | bytes 262160 | tf_op jit(solution)/shard_map/psum | solution.py:31
  455.9 14.5 %convolution_subtract_fusion = f32[8192,256]{1,0:T(8,128)} fusion(f32[8192,256]{1,0:T(8,128)} %param.3, f32[8192,256]{1,0:T(8,128)} %bitcast.44, f32[256,256]{1,0:T(8,128)} %all-reduce.6.cloned.1.call-done), kind=kOutput, calls=%fused_computation.2 | convolution fusion | flops 6444548096 | bytes 25427968 | tf_op jit(solution)/shard_map/dot_general | solution.py:9
  470.4 0.7 broadcast_multiply_fusion
  (30 shorter events, 2.7 us)
Async XLA Ops:
  7.2 1.6 copy-start
  7.2 151.0 %all-reduce.4.cloned.1.call-start = ((), (), s32[]{:S(2)}) async-start(), calls=%async_computation.1 | async-start | bytes 524288 | tf_op jit(solution)/shard_map/psum | solution.py:24
  12.9 442.9 %all-reduce.6.cloned.1.call-start = ((), (), s32[]{:S(2)}) async-start(), calls=%async_computation.2 | async-start | bytes 524288 | tf_op jit(solution)/shard_map/psum | solution.py:31
  239.2 102.2 %slice-start = ((s8[8388608]{0:T(1024)(128)(4,1)}), s8[4194304]{0:T(1024)(128)(4,1)S(1)}, s32[]{:S(2)}) async-start(s8[8388608]{0:T(1024)(128)(4,1)} %bitcast.45), calls=%async_computation.3 | async-start | bytes 8388608
  241.6 99.8 %slice-start.1 = ((s8[8388608]{0:T(1024)(128)(4,1)}), s8[4194304]{0:T(1024)(128)(4,1)S(1)}, s32[]{:S(2)}) async-start(s8[8388608]{0:T(1024)(128)(4,1)} %bitcast.45), calls=%async_computation.4 | async-start | bytes 8388608
  338.2 3.2 copy-start.1
  455.9 14.5 %copy-start.2 = (f32[256,256]{1,0:T(8,128)S(1)}, f32[256,256]{1,0:T(8,128)}, u32[]{:S(2)}) copy-start(f32[256,256]{1,0:T(8,128)} %all-reduce.6.cloned.1.call-done) | copy-start | bytes 786436
Sparse Core Ops, SparseCore 0:
  13.3 144.8 all-reduce.3
  356.3 99.5 all-reduce.5

commit v2 on v0

--- a/solution.py
+++ b/solution.py
@@ -26,7 +26,11 @@
     inverse = lower_inverse(lower)
     basis_part = matmul(panel_cols, inverse.T)
     orthonormal = lax.all_gather(basis_part, "cols", axis=0, tiled=True)
-    coupling = lax.psum(matmul(orthonormal.T, trailing), "rows")
+
+    def columns_trace(array_in):
+        return jnp.sum(lax.all_gather(array_in, "rows"), axis=0)
+
+    coupling = columns_trace(matmul(orthonormal.T, trailing))
     updated = trailing - matmul(orthonormal, coupling)
     return (lower.T * shrink, coupling * shrink, updated)
 

time: 447 us -> 401 us (0.90)
  waiting for transfers between devices: 327 us -> 279 us
    psum x1 -> x0, waiting for transfers between devices: 102 us -> none  [local(): coupling = lax.psum(matmul(orthonormal.T, trailing), 'rows')]
    all_gather x0 -> x1, waiting for transfers between devices: none -> 53.7 us  [columns_trace(): return jnp.sum(lax.all_gather(array_in, 'rows'), axis=0)]
where the time goes in v2:
time: 401 us
  waiting for transfers between devices  279 us (70%)
  other arithmetic  59.3 us (15%)
  matrix products  39 us (10%)
  between operations  15.2 us (4%)
  local copies, waits for them, and re-layouts  7.5 us (2%)
    psum x1, waiting for transfers between devices, local(): gram_sum = lax.psum(matmul(panel_cols.T, panel_cols), ('rows', 'cols'))  145 us
    all_gather x1, waiting for transfers between devices, local(): orthonormal = lax.all_gather(basis_part, 'cols', axis=0, tiled=True)  80.6 us
    all_gather x1, waiting for transfers between devices, columns_trace(): return jnp.sum(lax.all_gather(array_in, 'rows'), axis=0)  53.7 us
    dot_general x4, matrix products, matmul(): return jnp.dot(left, right, precision=lax.Precision.HIGHEST)  37.7 us
    another operation x6, other arithmetic, lower_factor(): return jnp.linalg.cholesky(gram_sum)  34 us
    another operation x3, other arithmetic, lower_inverse(): return jax.scipy.linalg.solve_triangular(lower, identity, lower=True)  19.7 us
  transfers between devices with their start and end apart: 3, of which 3 were waited for; matrix products, arithmetic and copies ran while one was open for 0% of the time, Pallas kernels for 0%

profile of v2, /device:TPU:1, one launch (start us, length us, event | category | flops | bytes accessed | tf_op | source)
XLA Modules:
  0.0 400.9 jit_solution(11327719766925225595)
XLA Ops:
  7.2 1.5 copy-done
  8.8 4.2 %fusion.14 = f32[256,256]{0,1:T(8,128)} fusion(f32[2048,256]{1,0:T(8,128)S(1)} %copy-done), kind=kOutput, calls=%fused_computation.38 | convolution fusion | flops 1610612736 | bytes 2359296 | tf_op jit(solution)/shard_map/dot_general | solution.py:9
  13.2 144.9 %all-reduce.3.cloned.1.call-done = f32[256,256]{0,1:T(8,128)} async-done(((f32[256,256]{0,1:T(8,128)}), f32[256,256]{0,1:T(8,128)}) %all-reduce.3.cloned.1.call-update) | async-done | bytes 262160 | tf_op jit(solution)/shard_map/psum | solution.py:24
  158.2 1.1 copy.6
  159.2 1.0 fusion.3
  160.2 11.7 %cholesky.50 = f32[128,128]{1,0:T(8,128)S(1)} custom-call(f32[128,128]{1,0:T(8,128)S(1)} %cholesky.118), custom_call_target="Cholesky" | custom-call | tf_op jit(solution)/shard_map/jit(cholesky)/cholesky | solution.py:13
  172.0 9.8 %custom-call.15 = f32[1,128,128]{1,2,0:T(8,128)S(1)} custom-call(f32[1,128,128]{2,1,0:T(8,128)S(1)} %get-tuple-element.29), custom_call_target="InvertDiagBlocksLowerTriangular" | custom-call | tf_op jit(solution)/shard_map/jit(cholesky)/cholesky | solution.py:13
  182.3 11.7 %cholesky.105 = f32[128,128]{1,0:T(8,128)S(1)} custom-call(f32[128,128]{1,0:T(8,128)S(1)} %convolution_subtract_fusion.2), custom_call_target="Cholesky" | custom-call | tf_op jit(solution)/shard_map/jit(cholesky)/cholesky | solution.py:13
  194.1 0.6 compare_reduce_fusion
  196.1 4.2 %while.1 = (s32[]{:T(128)}, f32[256,256]{1,0:T(8,128)S(1)}, s32[2,2]{1,0:T(2,128)S(1)}, f32[2,128,128]{2,1,0:T(8,128)S(1)}, s32[]{:T(128)}) while((s32[]{:T(128)}, f32[256,256]{1,0:T(8,128)S(1)}, s32[2,2]{1,0:T(2,128)S(1)}, f32[2,128,128]{2,1,0:T(8,128)S(1)}, s32[]{:T(128)}) %tuple.29), condition=%wide.while_cond, body=%wide.while_body.sunk | while | flops 2 | bytes 131189 | solution.py:18
  196.3 0.6 fusion.28
  196.9 1.4 bitcast_dynamic-update-slice_fusion.2
  198.3 0.6 fusion.28
  198.9 1.4 bitcast_dynamic-update-slice_fusion.2
  200.3 19.7 %custom-call.16 = f32[2,128,128]{1,2,0:T(8,128)S(1)} custom-call(f32[2,128,128]{2,1,0:T(8,128)S(1)} %get-tuple-element.10), custom_call_target="InvertDiagBlocksLowerTriangular" | custom-call | tf_op jit(solution)/shard_map/jit(_solve_triangular)/triangular_solve | solution.py:18
  220.5 0.3 fusion.8
  220.8 3.3 convolution_bitcast_fusion
  224.2 80.6 %all-gather.4.cloned.1.call-done = f32[8192,256]{0,1:T(8,128)} async-done(((f32[2048,256]{0,1:T(8,128)}), f32[8192,256]{0,1:T(8,128)}) %all-gather.4.cloned.1.call-update) | async-done | bytes 8388624 | tf_op jit(solution)/shard_map/all_gather | solution.py:28
  304.8 11.4 %fusion.15 = f32[256,256]{1,0:T(8,128)} fusion(f32[8192,256]{0,1:T(8,128)} %all-gather.4.cloned.1.call-done, f32[8192,256]{1,0:T(8,128)} %param.3), kind=kOutput, calls=%fused_computation.39 | convolution fusion | flops 6442450944 | bytes 17039360 | tf_op jit(solution)/shard_map/dot_general | solution.py:9
  316.2 0.8 copy.7
  317.1 53.7 %all-gather.6.cloned.1.call-done = f32[8192,256]{1,0:T(8,128)} async-done(((f32[256,256]{1,0:T(8,128)}), f32[8192,256]{1,0:T(8,128)}) %all-gather.6.cloned.1.call-update) | async-done | bytes 8388624 | tf_op jit(solution)/shard_map/all_gather | solution.py:31
  370.8 3.9 reduce_sum.9
  374.7 0.7 broadcast_multiply_fusion
  375.5 18.9 %convolution_subtract_fusion = f32[8192,256]{1,0:T(8,128)} fusion(f32[8192,256]{1,0:T(8,128)} %param.3, f32[8192,256]{0,1:T(8,128)} %all-gather.4.cloned.1.call-done, f32[256,256]{1,0:T(8,128)S(1)} %reduce_sum.9), kind=kOutput, calls=%fused_computation.2 | convolution fusion | flops 6444548096 | bytes 25427968 | tf_op jit(solution)/shard_map/dot_general | solution.py:9
  (22 shorter events, 1.6 us)
Async XLA Ops:
  7.2 1.6 copy-start
  7.2 151.0 %all-reduce.3.cloned.1.call-start = ((), (), s32[]{:S(2)}) async-start(), calls=%async_computation | async-start | bytes 524288 | tf_op jit(solution)/shard_map/psum | solution.py:24
  12.9 291.9 %all-gather.4.cloned.1.call-start = ((), (), s32[]{:S(2)}) async-start(), calls=%async_computation.1 | async-start | bytes 10485760 | tf_op jit(solution)/shard_map/all_gather | solution.py:28
  224.1 146.7 %all-gather.6.cloned.1.call-start = ((), (), s32[]{:S(2)}) async-start(), calls=%async_computation.2 | async-start | bytes 8650752 | tf_op jit(solution)/shard_map/all_gather | solution.py:31
Sparse Core Ops, SparseCore 0:
  13.3 144.7 all-reduce.2
  224.3 80.5 all-gather.3
  316.3 54.4 all-gather.5
